TPU v7x, 32 devices: a whole 2x2x4 slice. The times are simulated.
32 devices in a mesh: gx: 4 (over y, x), gy: 8 (over z, core).
Axes of the slice: x: 2, y: 2, z: 4, core: 2. Of those that a mesh axis runs over, the one named last changes fastest.
Arguments:
- tracer: float32 [6, 1024, 512], P(None, 'gy', 'gx'), may hold values from -6 to 6
- courant: float32 [2, 2, 1024, 512], P(None, None, 'gy', 'gx'), may hold values from 0.05 to 0.95
- displacement: int32 [2, 2, 8, 4], P(None, None, 'gy', 'gx'), may hold values from -16 to 16, as said below
- cotangent: float32 [6, 1024, 512], P(None, 'gy', 'gx'), may hold values from -6 to 6
Outputs:
- tracer_grad: float32 [6, 1024, 512], P(None, 'gy', 'gx')
- courant_grad: float32 [2, 2, 1024, 512], P(None, None, 'gy', 'gx')
Inputs may be any that keep to these rules, and one draw needn't show every extreme that they name: `displacement`: in every draw each of the two steps has a block with row and column offsets 16 and a block with row and column offsets -16.
All inputs are finite; a program needn't handle non-finite values.
Results may differ from a plain program's by a relative error of at most 0.0001.
Values sent between devices are 32-bit elements; how exact they have to be, the bound alone decides.
A program may use at most 64 MiB of HBM per device.

v0:
```python
import jax
import jax.numpy as jnp
from jax import lax
from jax.sharding import PartitionSpec as P

BLOCK = 128
REACH = 16


def padded_2(block, sides, width):
    for axis, dim in sides:
        count = lax.axis_size(axis)
        forward = [(i, i + 1) for i in range(count - 1)]
        forward.append((count - 1, 0))
        backward = [(target, source) for source, target in forward]
        low = lax.ppermute(
            lax.slice_in_dim(block, block.shape[dim] - width, None, axis=dim), axis, forward
        )
        high = lax.ppermute(lax.slice_in_dim(block, 0, width, axis=dim), axis, backward)
        block = jnp.concatenate([low, block, high], axis=dim)
    return block


def lagrange_weights(fraction):
    return (
        -fraction * (fraction - 1.0) * (fraction - 2.0) / 6.0,
        (fraction + 1.0) * (fraction - 1.0) * (fraction - 2.0) / 2.0,
        -(fraction + 1.0) * fraction * (fraction - 2.0) / 2.0,
        (fraction + 1.0) * fraction * (fraction - 1.0) / 6.0,
    )


def lagrange_slopes(fraction):
    square = fraction * fraction
    return (
        -(3.0 * square - 6.0 * fraction + 2.0) / 6.0,
        (3.0 * square - 4.0 * fraction - 1.0) / 2.0,
        -(3.0 * square - 2.0 * fraction - 2.0) / 2.0,
        (3.0 * square - 1.0) / 6.0,
    )


def to_blocks(values, side):
    leading = values.shape[:-2]
    block_rows = values.shape[-2] // side
    block_cols = values.shape[-1] // side
    reshaped = values.reshape(leading + (block_rows, side, block_cols, side))
    count = len(leading)
    ordering = (count, count + 2) + tuple(range(count)) + (count + 1, count + 3)
    return reshaped.transpose(ordering).reshape((block_rows * block_cols,) + leading + (side, side))


def from_blocks(blocked, block_rows, block_cols):
    side = blocked.shape[-1]
    leading = blocked.shape[1:-2]
    count = len(leading)
    reshaped = blocked.reshape((block_rows, block_cols) + leading + (side, side))
    ordering = tuple(range(2, 2 + count)) + (0, count + 2, 1, count + 3)
    return reshaped.transpose(ordering).reshape(leading + (block_rows * side, block_cols * side))


def block_starts(offsets, side, halo_width):
    block_rows, block_cols = (offsets.shape[1], offsets.shape[2])
    row_index = lax.broadcasted_iota(jnp.int32, (block_rows, block_cols), 0)
    col_index = lax.broadcasted_iota(jnp.int32, (block_rows, block_cols), 1)
    first_rows = (halo_width - 2 + row_index * side - offsets[0]).reshape(-1)
    first_cols = (halo_width - 2 + col_index * side - offsets[1]).reshape(-1)
    return (first_rows, first_cols)


def windows(padded, offsets, side, halo_width):
    first_rows, first_cols = block_starts(offsets, side, halo_width)
    tracers = padded.shape[0]

    def cutout(row_at, col_at):
        return lax.dynamic_slice(
            padded, (jnp.int32(0), row_at, col_at), (tracers, side + 3, side + 3)
        )

    return jax.vmap(cutout)(first_rows, first_cols)


def advect(padded, offsets, courant_pair, side, halo_width):
    block_rows, block_cols = (offsets.shape[1], offsets.shape[2])
    window_set = windows(padded, offsets, side, halo_width)
    row_weights = lagrange_weights(1.0 - to_blocks(courant_pair[0], side))
    col_weights = lagrange_weights(1.0 - to_blocks(courant_pair[1], side))
    running_sum = jnp.zeros(window_set.shape[:2] + (side, side), jnp.float32)
    for tap_row in range(4):
        for tap_col in range(4):
            factor = (row_weights[tap_row] * col_weights[tap_col])[:, None]
            running_sum = (
                running_sum
                + factor * window_set[:, :, tap_row : tap_row + side, tap_col : tap_col + side]
            )
    return from_blocks(running_sum, block_rows, block_cols)


def courant_sens(padded, offsets, courant_pair, adjoint, side, halo_width):
    block_rows, block_cols = (offsets.shape[1], offsets.shape[2])
    window_set = windows(padded, offsets, side, halo_width)
    row_fraction = 1.0 - to_blocks(courant_pair[0], side)
    col_fraction = 1.0 - to_blocks(courant_pair[1], side)
    row_weights = lagrange_weights(row_fraction)
    col_weights = lagrange_weights(col_fraction)
    row_slopes = lagrange_slopes(row_fraction)
    col_slopes = lagrange_slopes(col_fraction)
    along_rows = jnp.zeros(window_set.shape[:2] + (side, side), jnp.float32)
    along_cols = jnp.zeros(window_set.shape[:2] + (side, side), jnp.float32)
    for tap_row in range(4):
        for tap_col in range(4):
            tap_values = window_set[:, :, tap_row : tap_row + side, tap_col : tap_col + side]
            along_rows = (
                along_rows + (row_slopes[tap_row] * col_weights[tap_col])[:, None] * tap_values
            )
            along_cols = (
                along_cols + (row_weights[tap_row] * col_slopes[tap_col])[:, None] * tap_values
            )
    blocked_adjoint = to_blocks(adjoint, side)
    sens_rows = -jnp.sum(blocked_adjoint * along_rows, axis=1)
    sens_cols = -jnp.sum(blocked_adjoint * along_cols, axis=1)
    return jnp.stack(
        (
            from_blocks(sens_rows, block_rows, block_cols),
            from_blocks(sens_cols, block_rows, block_cols),
        )
    )


def spread(adjoint, offsets, courant_pair, side, halo_width):
    tracers, height, width = adjoint.shape
    blocked_adjoint = to_blocks(adjoint, side)
    row_weights = lagrange_weights(1.0 - to_blocks(courant_pair[0], side))
    col_weights = lagrange_weights(1.0 - to_blocks(courant_pair[1], side))
    pieces = jnp.zeros(blocked_adjoint.shape[:2] + (side + 3, side + 3), jnp.float32)
    for tap_row in range(4):
        for tap_col in range(4):
            factor = (row_weights[tap_row] * col_weights[tap_col])[:, None]
            pieces = pieces + jnp.pad(
                factor * blocked_adjoint,
                ((0, 0), (0, 0), (tap_row, 3 - tap_row), (tap_col, 3 - tap_col)),
            )
    first_rows, first_cols = block_starts(offsets, side, halo_width)

    def deposit(block_index, accumulator):
        corner = (jnp.int32(0), first_rows[block_index], first_cols[block_index])
        current = lax.dynamic_slice(accumulator, corner, (tracers, side + 3, side + 3))
        return lax.dynamic_update_slice(accumulator, current + pieces[block_index], corner)

    empty = jnp.zeros((tracers, height + 2 * halo_width, width + 2 * halo_width), jnp.float32)
    return lax.fori_loop(0, pieces.shape[0], deposit, empty)


def fold_columns(padded, halo_width):
    span_cols = padded.shape[2] - 2 * halo_width
    rim_pair = jnp.concatenate(
        (padded[:, :, :halo_width], padded[:, :, halo_width + span_cols :]), axis=2
    )
    extended = padded_2(rim_pair, (("gx", 2),), halo_width)
    interior = padded[:, :, halo_width : halo_width + span_cols]
    left = interior[:, :, :halo_width] + extended[:, :, :halo_width]
    right = interior[:, :, span_cols - halo_width :] + extended[:, :, 3 * halo_width :]
    return jnp.concatenate(
        (left, interior[:, :, halo_width : span_cols - halo_width], right), axis=2
    )


def fold_rows(padded, halo_width):
    span_rows = padded.shape[1] - 2 * halo_width
    rim_pair = jnp.concatenate(
        (padded[:, :halo_width], padded[:, halo_width + span_rows :]), axis=1
    )
    extended = padded_2(rim_pair, (("gy", 1),), halo_width)
    interior = padded[:, halo_width : halo_width + span_rows]
    upper = interior[:, :halo_width] + extended[:, :halo_width]
    lower = interior[:, span_rows - halo_width :] + extended[:, 3 * halo_width :]
    return jnp.concatenate((upper, interior[:, halo_width : span_rows - halo_width], lower), axis=1)


def unfold(padded, halo_width):
    return fold_rows(fold_columns(padded, halo_width), halo_width)


def fetch(values, halo_width):
    return padded_2(values, (("gy", 1), ("gx", 2)), halo_width)


def body(tracer, courant, displacement, cotangent):
    halo_width = REACH + 2
    side = BLOCK
    padded_start = fetch(tracer, halo_width)
    middle = advect(padded_start, displacement[0], courant[0], side, halo_width)
    padded_middle = fetch(middle, halo_width)
    sens_late = courant_sens(
        padded_middle, displacement[1], courant[1], cotangent, side, halo_width
    )
    middle_adjoint = unfold(
        spread(cotangent, displacement[1], courant[1], side, halo_width), halo_width
    )
    sens_early = courant_sens(
        padded_start, displacement[0], courant[0], middle_adjoint, side, halo_width
    )
    tracer_grad = unfold(
        spread(middle_adjoint, displacement[0], courant[0], side, halo_width), halo_width
    )
    return (tracer_grad, jnp.stack((sens_early, sens_late)))


def solution(mesh):
    in_specs = (
        P(None, "gy", "gx"),
        P(None, None, "gy", "gx"),
        P(None, None, "gy", "gx"),
        P(None, "gy", "gx"),
    )
    out_specs = (P(None, "gy", "gx"), P(None, None, "gy", "gx"))
    return jax.shard_map(body, mesh=mesh, in_specs=in_specs, out_specs=out_specs, check_vma=False)
```

profile of v0, /device:TPU:0, one launch (start us, length us, event | category | flops | bytes accessed | tf_op | source)
XLA Modules:
  0.0 138.0 jit_solution(4164927707388542386)
XLA Ops:
  0.6 1.8 %multiply_bitcast_fusion.79 = (f32[128,128]{1,0:T(8,128)}, f32[128,128]{1,0:T(8,128)S(1)}, f32[128,128]{1,0:T(8,128)S(1)}, f32[128,128]{1,0:T(8,128)S(1)}, f32[1...) fusion(f32[2,2,128,128]{3,2,1,0:T(8,128)} %param.5), kind=kLoop, calls=%fused_computation.168 | loop fusion | flops 1097728 | bytes 851968 | tf_op jit(solution)/shard_map/mul | solution.py:114
  7.6 2.7 %add_bitcast_fusion.1 = f32[6,131,131]{2,1,0:T(8,128)S(1)} fusion(f32[1,6,128,128]{3,2,1,0:T(8,128)S(1)} %get-tuple-element.109, f32[1,6,128,128]{3,2,1,0:T(8,128)S(1)} %get-tuple-element.95, f32[1,6,128,128]{3,2,1,0:T(8,128)S(1)} %get-tuple-element.96, f32[1,6,128,128]{3,2,1,0:T(8,128)S(1)} %get-tuple-element.97, ...), kind=kLoop, calls=%fused_computation.21 | loop fusion | flops 1544490 | bytes 6703320 | tf_op jit(solution)/shard_map/while/body/eval_jaxpr/squeeze | solution.py:148
  10.4 5.0 %dynamic_update_slice.8 = f32[6,164,164]{2,1,0:T(8,128)S(1)} dynamic-update-slice(f32[6,164,164]{2,1,0:T(8,128)S(1)} %broadcast.2168.clone, f32[6,131,131]{2,1,0:T(8,128)S(1)} %add_bitcast_fusion.1, s32[]{:T(128)} %constant.102.clone.1, s32[]{:T(128)S(6)} %select_n.42, s32[]{:T(128)S(6)} %select_n.43) | dynamic-update-slice | bytes 823732 | tf_op jit(solution)/shard_map/while/body/eval_jaxpr/dynamic_update_slice | solution.py:148
  15.4 1.0 slice.377
  16.4 5.6 %collective-permute-start = (f32[6,164,18]{2,1,0:T(8,128)}, f32[6,164,18]{2,1,0:T(8,128)S(1)}, u32[]{:S(2)}, u32[]{:S(2)}) collective-permute-start(f32[6,164,18]{2,1,0:T(8,128)} %slice.377), channel_id=1, source_target_pairs={{0,8},{8,16},{16,24},{24,0},{1,9},{9,17},{17,25},{25,1},{2,10},{10... | collective-permute-start | bytes 212552 | tf_op jit(solution)/shard_map/ppermute | solution.py:16
  22.7 3.5 %collective-permute-start.9 = (f32[6,18,128]{2,1,0:T(8,128)}, f32[6,18,128]{2,1,0:T(8,128)}, u32[]{:S(2)}, u32[]{:S(2)}) collective-permute-start(f32[6,18,128]{2,1,0:T(8,128)} %get-tuple-element.93), channel_id=1, source_target_pairs={{1,0},{2,1},{3,2},{4,3},{5,4},{6,5},{7,6},{0,7},{9,8},{10,9},{11,1... | collective-permute-start | bytes 165896 | tf_op jit(solution)/shard_map/ppermute | solution.py:19
  30.0 0.9 multiply_bitcast_fusion.71
  31.9 1.0 multiply_bitcast_fusion.63
  34.3 1.0 pad_maximum_fusion.2
  36.2 2.3 %collective-permute-start.11 = (f32[6,164,18]{2,1,0:T(8,128)S(1)}, f32[6,164,18]{2,1,0:T(8,128)S(1)}, u32[]{:S(2)}, u32[]{:S(2)}) collective-permute-start(f32[6,164,18]{2,1,0:T(8,128)S(1)} %get-tuple-element.72), channel_id=1, source_target_pairs={{8,0},{16,8},{24,16},{0,24},{9,1},{17,9},{25,17},{1,25},{10,2},{18... | collective-permute-start | bytes 212552 | tf_op jit(solution)/shard_map/ppermute | solution.py:19
  38.8 12.3 %collective-permute-done.10 = f32[6,164,18]{2,1,0:T(8,128)S(1)} collective-permute-done((f32[6,164,18]{2,1,0:T(8,128)S(1)}, f32[6,164,18]{2,1,0:T(8,128)S(1)}, u32[]{:S(2)}, u32[]{:S(2)}) %collective-permute-start.10) | collective-permute-done | bytes 70880 | tf_op jit(solution)/shard_map/ppermute | solution.py:16
  51.1 11.1 %collective-permute-done.11 = f32[6,164,18]{2,1,0:T(8,128)S(1)} collective-permute-done((f32[6,164,18]{2,1,0:T(8,128)S(1)}, f32[6,164,18]{2,1,0:T(8,128)S(1)}, u32[]{:S(2)}, u32[]{:S(2)}) %collective-permute-start.11) | collective-permute-done | bytes 70880 | tf_op jit(solution)/shard_map/ppermute | solution.py:19
  62.3 2.1 %fusion.7 = f32[1,6,131,131]{3,2,1,0:T(8,128)S(1)} fusion(s32[]{:T(128)} %bitcast.60, s32[]{:T(128)} %bitcast.62, f32[6,164,18]{2,1,0:T(8,128)S(1)} %collective-permute-done.10, f32[6,18,128]{2,1,0:T(8,128)} %collective-permute-done.8, f32[6,128,128]{2,1,0:T(8,128)S(1)} %copy-done.2, f32[6,18,128]{2,1,0:T(8,128)} %collective-permute-done.9, ...), kind=kLoop, calls=%fused_computation.17 | loop fusion | flops 411864 | bytes 1057376 | tf_op jit(solution)/shard_map/vmap()/gather | solution.py:76
  64.6 1.3 add_bitcast_fusion.2
  66.0 3.5 %collective-permute-start.13 = (f32[6,18,128]{2,1,0:T(8,128)S(1)}, f32[6,18,128]{2,1,0:T(8,128)S(1)}, u32[]{:S(2)}, u32[]{:S(2)}) collective-permute-start(f32[6,18,128]{2,1,0:T(8,128)S(1)} %get-tuple-element.91), channel_id=1, source_target_pairs={{1,0},{2,1},{3,2},{4,3},{5,4},{6,5},{7,6},{0,7},{9,8},{10,9},{11,1... | collective-permute-start | bytes 165896 | tf_op jit(solution)/shard_map/ppermute | solution.py:19
  69.5 1.0 collective-permute-done.1
  72.6 4.2 %collective-permute-done.2 = f32[6,18,128]{2,1,0:T(8,128)S(1)} collective-permute-done((f32[6,18,128]{2,1,0:T(8,128)S(1)}, f32[6,18,128]{2,1,0:T(8,128)S(1)}, u32[]{:S(2)}, u32[]{:S(2)}) %collective-permute-start.2) | collective-permute-done | bytes 55328 | tf_op jit(solution)/shard_map/ppermute | solution.py:16
  76.9 1.1 fusion.13
  78.5 2.4 %collective-permute-start.15 = (f32[6,164,18]{2,1,0:T(8,128)}, f32[6,164,18]{2,1,0:T(8,128)}, u32[]{:S(2)}, u32[]{:S(2)}) collective-permute-start(f32[6,164,18]{2,1,0:T(8,128)} %get-tuple-element.70), channel_id=1, source_target_pairs={{8,0},{16,8},{24,16},{0,24},{9,1},{17,9},{25,17},{1,25},{10,2},{18... | collective-permute-start | bytes 212552 | tf_op jit(solution)/shard_map/ppermute | solution.py:19
  81.8 3.6 %add_bitcast_fusion = f32[6,131,131]{2,1,0:T(8,128)} fusion(f32[1,6,128,128]{3,2,1,0:T(8,128)S(1)} %get-tuple-element.89, f32[1,6,128,128]{3,2,1,0:T(8,128)S(1)} %get-tuple-element.88, f32[1,6,128,128]{3,2,1,0:T(8,128)S(1)} %get-tuple-element.87, f32[1,6,128,128]{3,2,1,0:T(8,128)S(1)} %get-tuple-element.86, f32[1,6,128,128]{3,2,1,0:T(8,128)S(1)} %get-tuple-element.85, ...), kind=kLoop, calls=%fused_computation.20 | loop fusion | flops 1544490 | bytes 6703320 | tf_op jit(solution)/shard_map/while/body/eval_jaxpr/squeeze | solution.py:148
  85.5 7.8 %dynamic_update_slice.9 = f32[6,164,164]{2,1,0:T(8,128)S(1)} dynamic-update-slice(f32[6,164,164]{2,1,0:T(8,128)S(1)} %broadcast.2168, f32[6,131,131]{2,1,0:T(8,128)} %add_bitcast_fusion, s32[]{:T(128)} %constant.102.clone.1, s32[]{:T(128)S(6)} %select_n.44, s32[]{:T(128)S(6)} %select_n.45) | dynamic-update-slice | bytes 823732 | tf_op jit(solution)/shard_map/while/body/eval_jaxpr/dynamic_update_slice | solution.py:148
  93.7 1.2 collective-permute-start.4
  95.2 1.3 multiply_reduce_fusion.1
  96.6 1.3 multiply_reduce_fusion
  98.2 5.7 %collective-permute-done.15 = f32[6,164,18]{2,1,0:T(8,128)} collective-permute-done((f32[6,164,18]{2,1,0:T(8,128)}, f32[6,164,18]{2,1,0:T(8,128)}, u32[]{:S(2)}, u32[]{:S(2)}) %collective-permute-start.15) | collective-permute-done | bytes 70880 | tf_op jit(solution)/shard_map/ppermute | solution.py:19
  104.0 2.4 %fusion.2 = f32[1,6,131,131]{3,2,1,0:T(8,128)S(1)} fusion(s32[]{:T(128)} %bitcast.102, s32[]{:T(128)} %bitcast.104, f32[6,164,18]{2,1,0:T(8,128)} %collective-permute-done.14, f32[6,18,128]{2,1,0:T(8,128)S(1)} %copy-done.15, f32[6,128,128]{2,1,0:T(8,128)S(1)} %add_bitcast_fusion.2, f32[6,18,128]{2,1,0:T(8,128)S(1)} %copy-done.17, ...), kind=kLoop, calls=%fused_computation.12 | loop fusion | flops 411864 | bytes 1057376 | tf_op jit(solution)/shard_map/vmap()/gather | solution.py:76
  106.7 1.3 fusion.10
  108.2 1.3 fusion.11
  109.5 5.9 %collective-permute-done.4 = f32[6,164,18]{2,1,0:T(8,128)S(1)} collective-permute-done((f32[6,164,18]{2,1,0:T(8,128)S(1)}, f32[6,164,18]{2,1,0:T(8,128)S(1)}, u32[]{:S(2)}, u32[]{:S(2)}) %collective-permute-start.4) | collective-permute-done | bytes 70880 | tf_op jit(solution)/shard_map/ppermute | solution.py:16
  116.1 13.0 %collective-permute-done.5 = f32[6,164,18]{2,1,0:T(8,128)S(1)} collective-permute-done((f32[6,164,18]{2,1,0:T(8,128)S(1)}, f32[6,164,18]{2,1,0:T(8,128)S(1)}, u32[]{:S(2)}, u32[]{:S(2)}) %collective-permute-start.5) | collective-permute-done | bytes 70880 | tf_op jit(solution)/shard_map/ppermute | solution.py:19
  130.1 4.9 %collective-permute-done.6 = f32[6,18,128]{2,1,0:T(8,128)S(1)} collective-permute-done((f32[6,18,128]{2,1,0:T(8,128)S(1)}, f32[6,18,128]{2,1,0:T(8,128)S(1)}, u32[]{:S(2)}, u32[]{:S(2)}) %collective-permute-start.6) | collective-permute-done | bytes 55328 | tf_op jit(solution)/shard_map/ppermute | solution.py:16
  135.5 1.6 %collective-permute-done.7 = f32[6,18,128]{2,1,0:T(8,128)S(1)} collective-permute-done((f32[6,18,128]{2,1,0:T(8,128)S(1)}, f32[6,18,128]{2,1,0:T(8,128)S(1)}, u32[]{:S(2)}, u32[]{:S(2)}) %collective-permute-start.7) | collective-permute-done | bytes 55328 | tf_op jit(solution)/shard_map/ppermute | solution.py:19
  (226 shorter events, 18.1 us)
Async XLA Ops:
  4.1 2.7 %copy-start.1 = (f32[6,128,128]{2,1,0:T(8,128)S(1)}, f32[6,128,128]{2,1,0:T(8,128)}, u32[]{:S(2)}) copy-start(f32[6,128,128]{2,1,0:T(8,128)} %param.7) | copy-start | bytes 1179652
  15.4 6.6 %copy-start.2 = (f32[6,128,128]{2,1,0:T(8,128)S(1)}, f32[6,128,128]{2,1,0:T(8,128)}, u32[]{:S(2)}) copy-start(f32[6,128,128]{2,1,0:T(8,128)} %param.4) | copy-start | bytes 1179652
  16.4 22.1 %collective-permute-start = (f32[6,164,18]{2,1,0:T(8,128)}, f32[6,164,18]{2,1,0:T(8,128)S(1)}, u32[]{:S(2)}, u32[]{:S(2)}) collective-permute-start(f32[6,164,18]{2,1,0:T(8,128)} %slice.377), channel_id=1, source_target_pairs={{0,8},{8,16},{16,24},{24,0},{1,9},{9,17},{17,25},{25,1},{2,10},{10... | collective-permute-start | bytes 212552 | tf_op jit(solution)/shard_map/ppermute | solution.py:16
  22.7 11.6 %collective-permute-start.8 = (f32[6,18,128]{2,1,0:T(8,128)}, f32[6,18,128]{2,1,0:T(8,128)}, u32[]{:S(2)}, u32[]{:S(2)}) collective-permute-start(f32[6,18,128]{2,1,0:T(8,128)} %get-tuple-element.92), channel_id=1, source_target_pairs={{0,1},{1,2},{2,3},{3,4},{4,5},{5,6},{6,7},{7,0},{8,9},{9,10},{10,1... | collective-permute-start | bytes 165896 | tf_op jit(solution)/shard_map/ppermute | solution.py:16
  22.7 11.6 %collective-permute-start.9 = (f32[6,18,128]{2,1,0:T(8,128)}, f32[6,18,128]{2,1,0:T(8,128)}, u32[]{:S(2)}, u32[]{:S(2)}) collective-permute-start(f32[6,18,128]{2,1,0:T(8,128)} %get-tuple-element.93), channel_id=1, source_target_pairs={{1,0},{2,1},{3,2},{4,3},{5,4},{6,5},{7,6},{0,7},{9,8},{10,9},{11,1... | collective-permute-start | bytes 165896 | tf_op jit(solution)/shard_map/ppermute | solution.py:19
  35.5 15.6 %collective-permute-start.10 = (f32[6,164,18]{2,1,0:T(8,128)S(1)}, f32[6,164,18]{2,1,0:T(8,128)S(1)}, u32[]{:S(2)}, u32[]{:S(2)}) collective-permute-start(f32[6,164,18]{2,1,0:T(8,128)S(1)} %get-tuple-element.73), channel_id=1, source_target_pairs={{0,8},{8,16},{16,24},{24,0},{1,9},{9,17},{17,25},{25,1},{2,10},{10... | collective-permute-start | bytes 212552 | tf_op jit(solution)/shard_map/ppermute | solution.py:16
  36.2 26.1 %collective-permute-start.11 = (f32[6,164,18]{2,1,0:T(8,128)S(1)}, f32[6,164,18]{2,1,0:T(8,128)S(1)}, u32[]{:S(2)}, u32[]{:S(2)}) collective-permute-start(f32[6,164,18]{2,1,0:T(8,128)S(1)} %get-tuple-element.72), channel_id=1, source_target_pairs={{8,0},{16,8},{24,16},{0,24},{9,1},{17,9},{25,17},{1,25},{10,2},{18... | collective-permute-start | bytes 212552 | tf_op jit(solution)/shard_map/ppermute | solution.py:19
  38.7 31.8 %collective-permute-start.1 = (f32[6,164,18]{2,1,0:T(8,128)S(1)}, f32[6,164,18]{2,1,0:T(8,128)S(1)}, u32[]{:S(2)}, u32[]{:S(2)}) collective-permute-start(f32[6,164,18]{2,1,0:T(8,128)S(1)} %get-tuple-element.67), channel_id=1, source_target_pairs={{8,0},{16,8},{24,16},{0,24},{9,1},{17,9},{25,17},{1,25},{10,2},{18... | collective-permute-start | bytes 212552 | tf_op jit(solution)/shard_map/ppermute | solution.py:19
  65.9 6.0 %collective-permute-start.12 = (f32[6,18,128]{2,1,0:T(8,128)S(1)}, f32[6,18,128]{2,1,0:T(8,128)S(1)}, u32[]{:S(2)}, u32[]{:S(2)}) collective-permute-start(f32[6,18,128]{2,1,0:T(8,128)S(1)} %get-tuple-element.90), channel_id=1, source_target_pairs={{0,1},{1,2},{2,3},{3,4},{4,5},{5,6},{6,7},{7,0},{8,9},{9,10},{10,1... | collective-permute-start | bytes 165896 | tf_op jit(solution)/shard_map/ppermute | solution.py:16
  66.0 6.0 %collective-permute-start.13 = (f32[6,18,128]{2,1,0:T(8,128)S(1)}, f32[6,18,128]{2,1,0:T(8,128)S(1)}, u32[]{:S(2)}, u32[]{:S(2)}) collective-permute-start(f32[6,18,128]{2,1,0:T(8,128)S(1)} %get-tuple-element.91), channel_id=1, source_target_pairs={{1,0},{2,1},{3,2},{4,3},{5,4},{6,5},{7,6},{0,7},{9,8},{10,9},{11,1... | collective-permute-start | bytes 165896 | tf_op jit(solution)/shard_map/ppermute | solution.py:19
  71.1 5.6 %collective-permute-start.2 = (f32[6,18,128]{2,1,0:T(8,128)S(1)}, f32[6,18,128]{2,1,0:T(8,128)S(1)}, u32[]{:S(2)}, u32[]{:S(2)}) collective-permute-start(f32[6,18,128]{2,1,0:T(8,128)S(1)} %pad_maximum_fusion.10), channel_id=1, source_target_pairs={{0,1},{1,2},{2,3},{3,4},{4,5},{5,6},{6,7},{7,0},{8,9},{9,10},{10,1... | collective-permute-start | bytes 165896 | tf_op jit(solution)/shard_map/ppermute | solution.py:16
  76.9 4.1 %collective-permute-start.3 = (f32[6,18,128]{2,1,0:T(8,128)S(1)}, f32[6,18,128]{2,1,0:T(8,128)S(1)}, u32[]{:S(2)}, u32[]{:S(2)}) collective-permute-start(f32[6,18,128]{2,1,0:T(8,128)S(1)} %get-tuple-element.63), channel_id=1, source_target_pairs={{1,0},{2,1},{3,2},{4,3},{5,4},{6,5},{7,6},{0,7},{9,8},{10,9},{11,1... | collective-permute-start | bytes 165896 | tf_op jit(solution)/shard_map/ppermute | solution.py:19
  78.1 20.1 %collective-permute-start.14 = (f32[6,164,18]{2,1,0:T(8,128)}, f32[6,164,18]{2,1,0:T(8,128)}, u32[]{:S(2)}, u32[]{:S(2)}) collective-permute-start(f32[6,164,18]{2,1,0:T(8,128)} %get-tuple-element.71), channel_id=1, source_target_pairs={{0,8},{8,16},{16,24},{24,0},{1,9},{9,17},{17,25},{25,1},{2,10},{10... | collective-permute-start | bytes 212552 | tf_op jit(solution)/shard_map/ppermute | solution.py:16
  78.5 25.3 %collective-permute-start.15 = (f32[6,164,18]{2,1,0:T(8,128)}, f32[6,164,18]{2,1,0:T(8,128)}, u32[]{:S(2)}, u32[]{:S(2)}) collective-permute-start(f32[6,164,18]{2,1,0:T(8,128)} %get-tuple-element.70), channel_id=1, source_target_pairs={{8,0},{16,8},{24,16},{0,24},{9,1},{17,9},{25,17},{1,25},{10,2},{18... | collective-permute-start | bytes 212552 | tf_op jit(solution)/shard_map/ppermute | solution.py:19
  93.7 21.8 %collective-permute-start.4 = (f32[6,164,18]{2,1,0:T(8,128)S(1)}, f32[6,164,18]{2,1,0:T(8,128)S(1)}, u32[]{:S(2)}, u32[]{:S(2)}) collective-permute-start(f32[6,164,18]{2,1,0:T(8,128)S(1)} %slice.383), channel_id=1, source_target_pairs={{0,8},{8,16},{16,24},{24,0},{1,9},{9,17},{17,25},{25,1},{2,10},{10... | collective-permute-start | bytes 212552 | tf_op jit(solution)/shard_map/ppermute | solution.py:16
  98.0 5.9 %copy-start.15 = (f32[6,18,128]{2,1,0:T(8,128)S(1)}, f32[6,18,128]{2,1,0:T(8,128)}, u32[]{:S(2)}) copy-start(f32[6,18,128]{2,1,0:T(8,128)} %copy-done.14) | copy-start | bytes 165892
  98.0 5.9 %copy-start.17 = (f32[6,18,128]{2,1,0:T(8,128)S(1)}, f32[6,18,128]{2,1,0:T(8,128)}, u32[]{:S(2)}) copy-start(f32[6,18,128]{2,1,0:T(8,128)} %copy-done.16) | copy-start | bytes 165892
  103.9 2.6 %copy-start.33 = (f32[128,128]{1,0:T(8,128)S(1)}, f32[128,128]{1,0:T(8,128)}, u32[]{:S(2)}) copy-start(f32[128,128]{1,0:T(8,128)} %get-tuple-element.136) | copy-start | bytes 196612
  103.9 2.6 %copy-start.34 = (f32[128,128]{1,0:T(8,128)S(1)}, f32[128,128]{1,0:T(8,128)}, u32[]{:S(2)}) copy-start(f32[128,128]{1,0:T(8,128)} %get-tuple-element.138) | copy-start | bytes 196612
  103.9 2.6 %copy-start.35 = (f32[128,128]{1,0:T(8,128)S(1)}, f32[128,128]{1,0:T(8,128)}, u32[]{:S(2)}) copy-start(f32[128,128]{1,0:T(8,128)} %get-tuple-element.139) | copy-start | bytes 196612
  103.9 2.6 %copy-start.36 = (f32[128,128]{1,0:T(8,128)S(1)}, f32[128,128]{1,0:T(8,128)}, u32[]{:S(2)}) copy-start(f32[128,128]{1,0:T(8,128)} %get-tuple-element.140) | copy-start | bytes 196612
  103.9 2.6 %copy-start.37 = (f32[128,128]{1,0:T(8,128)S(1)}, f32[128,128]{1,0:T(8,128)}, u32[]{:S(2)}) copy-start(f32[128,128]{1,0:T(8,128)} %get-tuple-element.141) | copy-start | bytes 196612
  103.9 2.6 %copy-start.44 = (f32[128,128]{1,0:T(8,128)S(1)}, f32[128,128]{1,0:T(8,128)}, u32[]{:S(2)}) copy-start(f32[128,128]{1,0:T(8,128)} %get-tuple-element.156) | copy-start | bytes 196612
  103.9 2.6 %copy-start.45 = (f32[128,128]{1,0:T(8,128)S(1)}, f32[128,128]{1,0:T(8,128)}, u32[]{:S(2)}) copy-start(f32[128,128]{1,0:T(8,128)} %get-tuple-element.157) | copy-start | bytes 196612
  103.9 2.6 %copy-start.46 = (f32[128,128]{1,0:T(8,128)S(1)}, f32[128,128]{1,0:T(8,128)}, u32[]{:S(2)}) copy-start(f32[128,128]{1,0:T(8,128)} %get-tuple-element.158) | copy-start | bytes 196612
  103.9 2.6 %copy-start.47 = (f32[128,128]{1,0:T(8,128)S(1)}, f32[128,128]{1,0:T(8,128)}, u32[]{:S(2)}) copy-start(f32[128,128]{1,0:T(8,128)} %get-tuple-element.168) | copy-start | bytes 196612
  104.0 2.6 %copy-start.48 = (f32[128,128]{1,0:T(8,128)S(1)}, f32[128,128]{1,0:T(8,128)}, u32[]{:S(2)}) copy-start(f32[128,128]{1,0:T(8,128)} %get-tuple-element.169) | copy-start | bytes 196612
  104.0 2.6 %copy-start.49 = (f32[128,128]{1,0:T(8,128)S(1)}, f32[128,128]{1,0:T(8,128)}, u32[]{:S(2)}) copy-start(f32[128,128]{1,0:T(8,128)} %get-tuple-element.170) | copy-start | bytes 196612
  104.0 2.6 %copy-start.50 = (f32[128,128]{1,0:T(8,128)S(1)}, f32[128,128]{1,0:T(8,128)}, u32[]{:S(2)}) copy-start(f32[128,128]{1,0:T(8,128)} %get-tuple-element.181) | copy-start | bytes 196612
  115.7 13.4 %collective-permute-start.5 = (f32[6,164,18]{2,1,0:T(8,128)S(1)}, f32[6,164,18]{2,1,0:T(8,128)S(1)}, u32[]{:S(2)}, u32[]{:S(2)}) collective-permute-start(f32[6,164,18]{2,1,0:T(8,128)S(1)} %get-tuple-element.65), channel_id=1, source_target_pairs={{8,0},{16,8},{24,16},{0,24},{9,1},{17,9},{25,17},{1,25},{10,2},{18... | collective-permute-start | bytes 212552 | tf_op jit(solution)/shard_map/ppermute | solution.py:19
  129.3 5.6 %collective-permute-start.6 = (f32[6,18,128]{2,1,0:T(8,128)S(1)}, f32[6,18,128]{2,1,0:T(8,128)S(1)}, u32[]{:S(2)}, u32[]{:S(2)}) collective-permute-start(f32[6,18,128]{2,1,0:T(8,128)S(1)} %pad_maximum_fusion.8), channel_id=1, source_target_pairs={{0,1},{1,2},{2,3},{3,4},{4,5},{5,6},{6,7},{7,0},{8,9},{9,10},{10,1... | collective-permute-start | bytes 165896 | tf_op jit(solution)/shard_map/ppermute | solution.py:16
  135.1 2.0 %collective-permute-start.7 = (f32[6,18,128]{2,1,0:T(8,128)S(1)}, f32[6,18,128]{2,1,0:T(8,128)S(1)}, u32[]{:S(2)}, u32[]{:S(2)}) collective-permute-start(f32[6,18,128]{2,1,0:T(8,128)S(1)} %get-tuple-element.61), channel_id=1, source_target_pairs={{1,0},{2,1},{3,2},{4,3},{5,4},{6,5},{7,6},{0,7},{9,8},{10,9},{11,1... | collective-permute-start | bytes 165896 | tf_op jit(solution)/shard_map/ppermute | solution.py:19
  (67 other events, 110.5 us)
where the time goes:
time: 139 us; the launch traced here: 138 us
  waiting for transfers between devices  60.4 us (43%)
  other arithmetic  34 us (24%)
  starting transfers between devices  20.7 us (15%)
  local copies, waits for them, and re-layouts  18.2 us (13%)
  between operations  4.73 us (3%)
    ppermute x8, waiting for transfers between devices, padded_2(): lax.ppermute(lax.slice_in_dim(block, 0, width, axis=dim), axis, backward)  32.4 us
    ppermute x8, waiting for transfers between devices, padded_2(): lax.ppermute(lax.slice_in_dim(block, block.shape[dim] - width, None, axis...  28 us
    dynamic_update_slice x2, local copies, waits for them, and re-layouts, deposit(): lax.dynamic_update_slice(accumulator, current + pieces[block_index], corner)  12.8 us
    ppermute x8, starting transfers between devices, padded_2(): lax.ppermute(lax.slice_in_dim(block, 0, width, axis=dim), axis, backward)  12.5 us
    mul x9, other arithmetic, courant_sens(): (row_slopes[tap_row] * col_weights[tap_col])[:, None] * tap_values  8.93 us
    ppermute x8, starting transfers between devices, padded_2(): lax.ppermute(lax.slice_in_dim(block, block.shape[dim] - width, None, axis...  8.13 us
    squeeze x2, other arithmetic, deposit(): pieces[block_index]  6.27 us
    gather x2, other arithmetic, cutout(): lax.dynamic_slice(padded, (jnp.int32(0), row_at, col_at), (tracers, side...  4.55 us
  transfers between devices with their start and end apart: 16, of which 10 were waited for; matrix products, arithmetic and copies ran while one was open for 26% of the time, Pallas kernels for 0%

commit v1 on v0

v1 whole, which is shorter than its diff:
```python
import jax
import jax.numpy as jnp
from jax import lax
from jax.experimental import pallas as pl
from jax.experimental.pallas import tpu as pltpu
from jax.sharding import PartitionSpec as P

NT = 6
SIDE = 128
HALO = 24
TALL = SIDE + 2 * HALO
WIN = SIDE + 8
PITCH = 21
WIDE = 18
PAD = 40
DEEP = 216
MESH = pl.DeviceIdType.MESH


def lagrange_weights(t):
    return (
        t * (t - 1.0) * (t - 2.0) * (-1.0 / 6.0),
        (t + 1.0) * (t - 1.0) * (t - 2.0) * 0.5,
        (t + 1.0) * t * (t - 2.0) * -0.5,
        (t + 1.0) * t * (t - 1.0) * (1.0 / 6.0),
    )


def lagrange_slopes(t):
    s = t * t
    return (
        (3.0 * s - 6.0 * t + 2.0) * (-1.0 / 6.0),
        (3.0 * s - 4.0 * t - 1.0) * 0.5,
        (3.0 * s - 2.0 * t - 2.0) * -0.5,
        (3.0 * s - 1.0) * (1.0 / 6.0),
    )


def kernel(
    sizes, tracer, courant, disp, cotangent, grad, sens,
    q0, q1, s, c0, c1, w, lap, vp, eb, hb, f, fp, ma, rr, rc, rx, send, recv,
):
    nx, ny = sizes
    q, c = (q0, q1), (c0, c1)
    ix, iy = lax.axis_index("gx"), lax.axis_index("gy")
    left, right = lax.rem(ix + nx - 1, nx), lax.rem(ix + 1, nx)
    up, down = lax.rem(iy + ny - 1, ny), lax.rem(iy + 1, ny)

    barrier = pltpu.get_barrier_semaphore()
    around = (
        (left, iy), (right, iy), (ix, up), (ix, down),
        (left, up), (left, down), (right, up), (right, down),
    )
    for who in around:
        pl.semaphore_signal(barrier, inc=1, device_id=who, device_id_type=MESH)

    lane = lax.broadcasted_iota(jnp.int32, (8, SIDE), 1)
    top, main, low = pl.ds(0, HALO), pl.ds(HALO, SIDE), pl.ds(HALO + SIDE, HALO)
    first, last = pl.ds(0, HALO), pl.ds(SIDE - HALO, HALO)

    def rows(k, shift=0):
        return pl.ds(pl.multiple_of(k * 8, 8) + shift, 8)

    def make(stage, plan):
        return [
            pltpu.make_async_remote_copy(
                src_ref=src, dst_ref=dst,
                send_sem=send.at[stage, n], recv_sem=recv.at[stage, n],
                device_id=who, device_id_type=MESH,
            )
            for n, (src, dst, who) in enumerate(plan)
        ]

    def halo_copies(h):
        return make(h, (
            (s.at[h, 0], c[h].at[0, main], (left, iy)),
            (s.at[h, 1], c[h].at[1, main], (right, iy)),
            (s.at[h, 0, first], c[h].at[0, low], (left, up)),
            (s.at[h, 0, last], c[h].at[0, top], (left, down)),
            (s.at[h, 1, first], c[h].at[1, low], (right, up)),
            (s.at[h, 1, last], c[h].at[1, top], (right, down)),
            (q[h].at[:, pl.ds(HALO, HALO)], q[h].at[:, low], (ix, up)),
            (q[h].at[:, pl.ds(SIDE, HALO)], q[h].at[:, top], (ix, down)),
        ))

    def fold_copies(x):
        return make(2 + x, (
            (fp.at[x, 0, main], rc.at[x, 0], (right, iy)),
            (fp.at[x, 1, main], rc.at[x, 1], (left, iy)),
            (fp.at[x, 0, top], rx.at[x, 0, 0], (right, up)),
            (fp.at[x, 0, low], rx.at[x, 0, 1], (right, down)),
            (fp.at[x, 1, top], rx.at[x, 1, 0], (left, up)),
            (fp.at[x, 1, low], rx.at[x, 1, 1], (left, down)),
            (f.at[x, :, top], rr.at[x, 0], (ix, up)),
            (f.at[x, :, low], rr.at[x, 1], (ix, down)),
        ))

    right_lanes = [(lane >= PITCH * t) & (lane < PITCH * t + WIDE) for t in range(NT)]
    left_lanes = [
        (lane >= (PITCH * t - WIDE) % SIDE) & (lane < (PITCH * t - WIDE) % SIDE + WIDE)
        for t in range(NT)
    ]

    def turned(value, amount):
        return value if amount % SIDE == 0 else pltpu.roll(value, amount % SIDE, 1)

    def pack(values):
        near_low = jnp.zeros((8, SIDE), jnp.float32)
        near_high = near_low
        for t in range(NT):
            moved = turned(values[t], PITCH * t)
            near_low = jnp.where(right_lanes[t], moved, near_low)
            near_high = jnp.where(left_lanes[t], moved, near_high)
        return near_low, near_high

    def geometry(step):
        dy, dx = disp[step, 0, 0, 0], disp[step, 1, 0, 0]
        base = -2 - dx
        shifts = [base + b for b in range(4)]
        masks = [(lane >= v) & (lane < SIDE + v) for v in shifts]
        return dy, base, shifts, masks

    def fractions(step, k):
        return 1.0 - courant[step, 0, rows(k), :], 1.0 - courant[step, 1, rows(k), :]

    def make_windows(step):
        dy, base, shifts, masks = geometry(step)
        start = HALO - 2 - dy
        border = (lax.rem(lane, PITCH) < 3) & (lane < PITCH * NT)
        lim = jnp.where(border, -3, 0)
        take_low = lim <= base
        turns = [lax.rem(SIDE - v, SIDE) for v in shifts]

        def block(k, _):
            at = pl.ds(start + k * 8, 8)
            merged = jnp.where(take_low, c[step][0, at, :], c[step][1, at, :])
            for t in range(NT):
                side = turned(merged, -PITCH * t)
                mid = q[step][t, at, :]
                for b in range(4):
                    w[b, t, rows(k), :] = pltpu.roll(jnp.where(masks[b], mid, side), turns[b], 1)
            return 0

        lax.fori_loop(0, WIN // 8, block, 0)

    def advect():
        def block(k, _):
            ty, tx = fractions(0, k)
            la, lb = lagrange_weights(ty), lagrange_weights(tx)
            done = []
            for t in range(NT):
                total = None
                for a in range(4):
                    line = lb[0] * w[0, t, rows(k, a), :]
                    for b in range(1, 4):
                        line = line + lb[b] * w[b, t, rows(k, a), :]
                    total = la[a] * line if total is None else total + la[a] * line
                q1[t, rows(k, HALO), :] = total
                done.append(total)
            s[1, 0, rows(k), :], s[1, 1, rows(k), :] = pack(done)
            return 0

        lax.fori_loop(0, SIDE // 8, block, 0)

    def sensitivity(step, g):
        def block(k, _):
            ty, tx = fractions(step, k)
            la, lb = lagrange_weights(ty), lagrange_weights(tx)
            da, db = lagrange_slopes(ty), lagrange_slopes(tx)
            gs = [g[t, rows(k), :] for t in range(NT)]
            along_rows = along_cols = None
            for a in range(4):
                line = slope = None
                for b in range(4):
                    tap = gs[0] * w[b, 0, rows(k, a), :]
                    for t in range(1, NT):
                        tap = tap + gs[t] * w[b, t, rows(k, a), :]
                    line = lb[b] * tap if line is None else line + lb[b] * tap
                    slope = db[b] * tap if slope is None else slope + db[b] * tap
                along_rows = da[a] * line if along_rows is None else along_rows + da[a] * line
                along_cols = la[a] * slope if along_cols is None else along_cols + la[a] * slope
            sens[step, 0, rows(k), :] = -along_rows
            sens[step, 1, rows(k), :] = -along_cols
            return 0

        lax.fori_loop(0, SIDE // 8, block, 0)

    def spread(step, g, x):
        dy, base, shifts, masks = geometry(step)
        turns = [lax.rem(SIDE + v, SIDE) for v in shifts]

        def weigh(k, _):
            ty, tx = fractions(step, k)
            la, lb = lagrange_weights(ty), lagrange_weights(tx)
            for a in range(4):
                lap[a, rows(k, 8), :] = la[a]
            for t in range(NT):
                value = g[t, rows(k), :]
                for b in range(4):
                    vp[b, t, rows(k, 8), :] = lb[b] * value
            return 0

        lax.fori_loop(0, SIDE // 8, weigh, 0)

        def deposit(k, _):
            la = [lap[a, rows(k, 8 - a), :] for a in range(4)]
            rims = []
            for t in range(NT):
                mid = rim = jnp.zeros((8, SIDE), jnp.float32)
                for b in range(4):
                    total = la[0] * vp[b, t, rows(k, 8), :]
                    for a in range(1, 4):
                        total = total + la[a] * vp[b, t, rows(k, 8 - a), :]
                    moved = pltpu.roll(total, turns[b], 1)
                    mid = mid + jnp.where(masks[b], moved, 0.0)
                    rim = rim + jnp.where(masks[b], 0.0, moved)
                eb[t, rows(k, PAD), :] = mid
                rims.append(rim)
            hb[0, rows(k, PAD), :], hb[1, rows(k, PAD), :] = pack(rims)
            return 0

        lax.fori_loop(0, WIN // 8, deposit, 0)
        start = PAD - HALO + 2 + dy

        def place(k, _):
            at = pl.ds(start + k * 8, 8)
            for t in range(NT):
                f[x, t, rows(k), :] = eb[t, at, :]
            for d in range(2):
                fp[x, d, rows(k), :] = hb[d, at, :]
            return 0

        lax.fori_loop(0, TALL // 8, place, 0)

    def fold(x, out):
        for d in range(2):
            rc[x, d, last, :] += rx[x, d, 0]
            rc[x, d, first, :] += rx[x, d, 1]
        for t in range(NT):
            f[x, t, pl.ds(SIDE, HALO), :] += rr[x, 0, t]
            f[x, t, pl.ds(HALO, HALO), :] += rr[x, 1, t]

        def block(k, _):
            from_left, from_right = rc[x, 0, rows(k), :], rc[x, 1, rows(k), :]
            for t in range(NT):
                low_part = turned(jnp.where(right_lanes[t], from_left, 0.0), -PITCH * t)
                high_part = turned(jnp.where(left_lanes[t], from_right, 0.0), -PITCH * t)
                out[t, rows(k), :] = f[x, t, rows(k, HALO), :] + low_part + high_part
            return 0

        lax.fori_loop(0, SIDE // 8, block, 0)

    def first_pack(k, _):
        values = [tracer[t, rows(k), :] for t in range(NT)]
        for t in range(NT):
            q0[t, rows(k, HALO), :] = values[t]
        s[0, 0, rows(k), :], s[0, 1, rows(k), :] = pack(values)
        return 0

    lax.fori_loop(0, SIDE // 8, first_pack, 0)
    pl.semaphore_wait(barrier, 8)
    halo0 = halo_copies(0)
    for copy in halo0:
        copy.start()

    lap[:, 0:8, :] = jnp.zeros((4, 8, SIDE), jnp.float32)
    lap[:, SIDE + 8:, :] = jnp.zeros((4, 8, SIDE), jnp.float32)
    vp[:, :, 0:8, :] = jnp.zeros((4, NT, 8, SIDE), jnp.float32)
    vp[:, :, SIDE + 8:, :] = jnp.zeros((4, NT, 8, SIDE), jnp.float32)
    eb[:, 0:PAD, :] = jnp.zeros((NT, PAD, SIDE), jnp.float32)
    eb[:, PAD + WIN:, :] = jnp.zeros((NT, DEEP - PAD - WIN, SIDE), jnp.float32)
    hb[:, 0:PAD, :] = jnp.zeros((2, PAD, SIDE), jnp.float32)
    hb[:, PAD + WIN:, :] = jnp.zeros((2, DEEP - PAD - WIN, SIDE), jnp.float32)

    spread(1, cotangent, 0)
    fold0 = fold_copies(0)
    for copy in fold0:
        copy.start()

    for copy in halo0:
        copy.wait_recv()
    make_windows(0)
    advect()
    halo1 = halo_copies(1)
    for copy in halo1:
        copy.start()

    for copy in fold0:
        copy.wait()
    fold(0, ma)
    spread(0, ma, 1)
    fold1 = fold_copies(1)
    for copy in fold1:
        copy.start()
    sensitivity(0, ma)

    for copy in halo1:
        copy.wait_recv()
    make_windows(1)
    sensitivity(1, cotangent)

    for copy in fold1:
        copy.wait()
    fold(1, grad)
    for copy in halo0 + halo1:
        copy.wait_send()


def solution(mesh):
    sizes = (mesh.shape["gx"], mesh.shape["gy"])
    f32 = jnp.float32

    def body(tracer, courant, displacement, cotangent):
        vmem = pl.BlockSpec(memory_space=pltpu.VMEM)
        return pl.pallas_call(
            lambda *refs: kernel(sizes, *refs),
            out_shape=(
                jax.ShapeDtypeStruct((NT, SIDE, SIDE), f32),
                jax.ShapeDtypeStruct((2, 2, SIDE, SIDE), f32),
            ),
            in_specs=[vmem, vmem, pl.BlockSpec(memory_space=pltpu.SMEM), vmem],
            out_specs=(vmem, vmem),
            scratch_shapes=[
                pltpu.VMEM((NT, TALL, SIDE), f32),
                pltpu.VMEM((NT, TALL, SIDE), f32),
                pltpu.VMEM((2, 2, SIDE, SIDE), f32),
                pltpu.VMEM((2, TALL, SIDE), f32),
                pltpu.VMEM((2, TALL, SIDE), f32),
                pltpu.VMEM((4, NT, WIN, SIDE), f32),
                pltpu.VMEM((4, SIDE + 16, SIDE), f32),
                pltpu.VMEM((4, NT, SIDE + 16, SIDE), f32),
                pltpu.VMEM((NT, DEEP, SIDE), f32),
                pltpu.VMEM((2, DEEP, SIDE), f32),
                pltpu.VMEM((2, NT, TALL, SIDE), f32),
                pltpu.VMEM((2, 2, TALL, SIDE), f32),
                pltpu.VMEM((NT, SIDE, SIDE), f32),
                pltpu.VMEM((2, 2, NT, HALO, SIDE), f32),
                pltpu.VMEM((2, 2, SIDE, SIDE), f32),
                pltpu.VMEM((2, 2, 2, HALO, SIDE), f32),
                pltpu.SemaphoreType.DMA((4, 8)),
                pltpu.SemaphoreType.DMA((4, 8)),
            ],
            compiler_params=pltpu.CompilerParams(
                collective_id=0, has_side_effects=True, vmem_limit_bytes=48 * 1024 * 1024
            ),
        )(tracer, courant, displacement, cotangent)

    in_specs = (
        P(None, "gy", "gx"),
        P(None, None, "gy", "gx"),
        P(None, None, "gy", "gx"),
        P(None, "gy", "gx"),
    )
    out_specs = (P(None, "gy", "gx"), P(None, None, "gy", "gx"))
    return jax.shard_map(body, mesh=mesh, in_specs=in_specs, out_specs=out_specs, check_vma=False)
```

time: 139 us -> 35 us (0.25)
  waiting for transfers between devices: 60.4 us -> 0 us
  other arithmetic: 34 us -> 0 us
  Pallas kernels: 0 us -> 28.9 us
  starting transfers between devices: 20.7 us -> 0 us
  local copies, waits for them, and re-layouts: 18.2 us -> 5.16 us
  between operations: 4.73 us -> 0.64 us
    ppermute x16 -> x0, waiting for transfers between devices: 60.4 us -> none  [the longest x8 32.4 us: padded_2(): lax.ppermute(lax.slice_in_dim(block, 0, width, axis=dim), axis, backward)]
    pallas_call x0 -> x1, Pallas kernels: none -> 28.9 us  [body(): pl.pallas_call(lambda *refs: kernel(sizes, *refs), out_shape=(jax.ShapeDt...]
    ppermute x16 -> x0, starting transfers between devices: 20.7 us -> none  [the longest x8 12.5 us: padded_2(): lax.ppermute(lax.slice_in_dim(block, 0, width, axis=dim), axis, backward)]
    dynamic_update_slice x2 -> x0, local copies, waits for them, and re-layouts: 12.8 us -> none  [deposit(): lax.dynamic_update_slice(accumulator, current + pieces[block_index], corner)]
    mul x16 -> x0, other arithmetic: 12.2 us -> none  [the longest x9 8.93 us: courant_sens(): (row_slopes[tap_row] * col_weights[tap_col])[:, None] * tap_values]
    squeeze x2 -> x0, other arithmetic: 6.27 us -> none  [deposit(): pieces[block_index]]
    reduce_sum x4 -> x0, other arithmetic: 5.19 us -> none  [the longest x2 2.6 us: courant_sens(): sens_rows = -jnp.sum(blocked_adjoint * along_rows, axis=1)]
    gather x2 -> x0, other arithmetic: 4.55 us -> none  [cutout(): lax.dynamic_slice(padded, (jnp.int32(0), row_at, col_at), (tracers, side...]
  transfers between devices with their start and end apart: 16 -> 0, of which waited for: 10 -> 0; matrix products, arithmetic and copies ran while one was open for 26% -> 0% of each run, Pallas kernels for 0% -> 0%
where the time goes in v1:
time: 35 us; the launch traced here: 34.7 us
  Pallas kernels  28.9 us (83%)
  local copies, waits for them, and re-layouts  5.16 us (15%)
  between operations  0.64 us (2%)
    pallas_call x1, Pallas kernels, body(): pl.pallas_call(lambda *refs: kernel(sizes, *refs), out_shape=(jax.ShapeDt...  28.9 us
    unnamed x9, local copies, waits for them, and re-layouts  5.16 us

profile of v1, /device:TPU:0, one launch (start us, length us, event | category | flops | bytes accessed | tf_op | source)
XLA Modules:
  0.0 34.7 jit_solution(4336618505832983780)
XLA Ops:
  0.6 0.8 %copy.6.refs_2_ = s32[2,2,1,1]{3,2,1,0:T(1,128)S(1)} copy(s32[2,2,1,1]{1,3,2,0:T(1,128)} %param.6) | data formatting | bytes 32 | tf_op args[2]
  1.4 0.0 copy-start
  1.4 1.0 %copy-done = f32[6,128,128]{2,1,0:T(8,128)S(1)} copy-done((f32[6,128,128]{2,1,0:T(8,128)S(1)}, f32[6,128,128]{2,1,0:T(8,128)}, u32[]{:S(2)}) %copy-start) | copy-done | bytes 393240
  2.4 0.0 copy-start.1
  2.4 1.0 %copy-done.1 = f32[6,128,128]{2,1,0:T(8,128)S(1)} copy-done((f32[6,128,128]{2,1,0:T(8,128)S(1)}, f32[6,128,128]{2,1,0:T(8,128)}, u32[]{:S(2)}) %copy-start.1) | copy-done | bytes 393240
  3.4 0.0 copy-start.2
  3.4 0.9 %copy-done.2 = f32[2,2,128,128]{3,2,1,0:T(8,128)S(1)} copy-done((f32[2,2,128,128]{3,2,1,0:T(8,128)S(1)}, f32[2,2,128,128]{3,2,1,0:T(8,128)}, u32[]{:S(2)}) %copy-start.2) | copy-done | bytes 262168
  4.3 28.9 %shard_map.59 = (f32[6,128,128]{2,1,0:T(8,128)S(1)}, f32[2,2,128,128]{3,2,1,0:T(8,128)S(1)}) custom-call(f32[6,128,128]{2,1,0:T(8,128)S(1)} %copy-done, f32[2,2,128,128]{3,2,1,0:T(8,128)S(1)} %copy-done.2, s32[2,2,1,1]{3,2,1,0:T(1,128)S(1)} %copy.6.refs_2_, f32[6,128,128]{2,1,0:T(8,128)S(1)} %copy-done.1), custom_call_target="tpu_custom_call" | custom-call | tf_op jit(solution)/shard_map/pallas_call | solution.py:315
  33.3 0.7 %copy.9 = f32[6,128,128]{2,1,0:T(8,128)} copy(f32[6,128,128]{2,1,0:T(8,128)S(1)} %get-tuple-element.4) | data formatting | bytes 786432
  34.0 0.7 %copy.10 = f32[2,2,128,128]{3,2,1,0:T(8,128)} copy(f32[2,2,128,128]{3,2,1,0:T(8,128)S(1)} %get-tuple-element.5) | data formatting | bytes 524288
Async XLA Ops:
  1.4 1.0 %copy-start = (f32[6,128,128]{2,1,0:T(8,128)S(1)}, f32[6,128,128]{2,1,0:T(8,128)}, u32[]{:S(2)}) copy-start(f32[6,128,128]{2,1,0:T(8,128)} %refs_0_.1) | copy-start | bytes 1179652
  2.4 1.0 %copy-start.1 = (f32[6,128,128]{2,1,0:T(8,128)S(1)}, f32[6,128,128]{2,1,0:T(8,128)}, u32[]{:S(2)}) copy-start(f32[6,128,128]{2,1,0:T(8,128)} %refs_3_.1) | copy-start | bytes 1179652
  3.4 0.9 %copy-start.2 = (f32[2,2,128,128]{3,2,1,0:T(8,128)S(1)}, f32[2,2,128,128]{3,2,1,0:T(8,128)}, u32[]{:S(2)}) copy-start(f32[2,2,128,128]{3,2,1,0:T(8,128)} %refs_1_.1) | copy-start | bytes 786436

commit v2 on v1

--- a/solution.py
+++ b/solution.py
@@ -37,14 +37,26 @@
 
 
 def kernel(
-    sizes, tracer, courant, disp, cotangent, grad, sens,
-    q0, q1, s, c0, c1, w, lap, vp, eb, hb, f, fp, ma, rr, rc, rx, send, recv,
+    sizes, tracer_in, courant_in, disp_in, cotangent_in, grad, sens,
+    courant, disp, cotangent, q0, q1, s, c0, c1, w, lap, vp, eb, hb, f, fp, ma, rr, rc, rx, send, recv, load,
 ):
     nx, ny = sizes
     q, c = (q0, q1), (c0, c1)
     ix, iy = lax.axis_index("gx"), lax.axis_index("gy")
     left, right = lax.rem(ix + nx - 1, nx), lax.rem(ix + 1, nx)
     up, down = lax.rem(iy + ny - 1, ny), lax.rem(iy + 1, ny)
+
+    loads = [
+        pltpu.make_async_copy(src, dst, load.at[n])
+        for n, (src, dst) in enumerate((
+            (tracer_in, q0.at[:, pl.ds(HALO, SIDE)]),
+            (disp_in, disp),
+            (courant_in, courant),
+            (cotangent_in, cotangent),
+        ))
+    ]
+    for copy in loads:
+        copy.start()
 
     barrier = pltpu.get_barrier_semaphore()
     around = (
@@ -114,7 +126,7 @@
         return near_low, near_high
 
     def geometry(step):
-        dy, dx = disp[step, 0, 0, 0], disp[step, 1, 0, 0]
+        dy, dx = disp[step, 0, 0, 0], disp[step, 0, 0, 1]
         base = -2 - dx
         shifts = [base + b for b in range(4)]
         masks = [(lane >= v) & (lane < SIDE + v) for v in shifts]
@@ -251,12 +263,11 @@
         lax.fori_loop(0, SIDE // 8, block, 0)
 
     def first_pack(k, _):
-        values = [tracer[t, rows(k), :] for t in range(NT)]
-        for t in range(NT):
-            q0[t, rows(k, HALO), :] = values[t]
+        values = [q0[t, rows(k, HALO), :] for t in range(NT)]
         s[0, 0, rows(k), :], s[0, 1, rows(k), :] = pack(values)
         return 0
 
+    loads[0].wait()
     lax.fori_loop(0, SIDE // 8, first_pack, 0)
     pl.semaphore_wait(barrier, 8)
     halo0 = halo_copies(0)
@@ -272,6 +283,8 @@
     hb[:, 0:PAD, :] = jnp.zeros((2, PAD, SIDE), jnp.float32)
     hb[:, PAD + WIN:, :] = jnp.zeros((2, DEEP - PAD - WIN, SIDE), jnp.float32)
 
+    for copy in loads[1:]:
+        copy.wait()
     spread(1, cotangent, 0)
     fold0 = fold_copies(0)
     for copy in fold0:
@@ -318,9 +331,12 @@
                 jax.ShapeDtypeStruct((NT, SIDE, SIDE), f32),
                 jax.ShapeDtypeStruct((2, 2, SIDE, SIDE), f32),
             ),
-            in_specs=[vmem, vmem, pl.BlockSpec(memory_space=pltpu.SMEM), vmem],
+            in_specs=[pl.BlockSpec(memory_space=pl.ANY)] * 4,
             out_specs=(vmem, vmem),
             scratch_shapes=[
+                pltpu.VMEM((2, 2, SIDE, SIDE), f32),
+                pltpu.SMEM((2, 1, 1, 2), jnp.int32),
+                pltpu.VMEM((NT, SIDE, SIDE), f32),
                 pltpu.VMEM((NT, TALL, SIDE), f32),
                 pltpu.VMEM((NT, TALL, SIDE), f32),
                 pltpu.VMEM((2, 2, SIDE, SIDE), f32),
@@ -339,11 +355,12 @@
                 pltpu.VMEM((2, 2, 2, HALO, SIDE), f32),
                 pltpu.SemaphoreType.DMA((4, 8)),
                 pltpu.SemaphoreType.DMA((4, 8)),
+                pltpu.SemaphoreType.DMA((4,)),
             ],
             compiler_params=pltpu.CompilerParams(
-                collective_id=0, has_side_effects=True, vmem_limit_bytes=48 * 1024 * 1024
+                collective_id=0, has_side_effects=True, vmem_limit_bytes=62 * 1024 * 1024
             ),
-        )(tracer, courant, displacement, cotangent)
+        )(tracer, courant, displacement.transpose(0, 2, 3, 1), cotangent)
 
     in_specs = (
         P(None, "gy", "gx"),

time: 35 us -> 32.6 us (0.931)
  local copies, waits for them, and re-layouts: 5.16 us -> 2.52 us
    unnamed x9 -> x4, local copies, waits for them, and re-layouts: 5.16 us -> 2.52 us
where the time goes in v2:
time: 32.6 us; the launch traced here: 32.4 us
  Pallas kernels  29.2 us (90%)
  local copies, waits for them, and re-layouts  2.52 us (8%)
  between operations  0.65 us (2%)
    pallas_call x1, Pallas kernels, body(): pl.pallas_call(lambda *refs: kernel(sizes, *refs), out_shape=(jax.ShapeDt...  29.2 us
    unnamed x4, local copies, waits for them, and re-layouts  2.52 us

profile of v2, /device:TPU:0, one launch (start us, length us, event | category | flops | bytes accessed | tf_op | source)
XLA Modules:
  0.0 32.4 jit_solution(1921830413656800250)
XLA Ops:
  0.6 29.2 %shard_map.59 = (f32[6,128,128]{2,1,0:T(8,128)}, f32[2,2,128,128]{3,2,1,0:T(8,128)}) custom-call(f32[6,128,128]{2,1,0:T(8,128)} %refs_0_.1, f32[2,2,128,128]{3,2,1,0:T(8,128)} %refs_1_.1, s32[2,1,1,2]{3,2,1,0:T(1,128)} %bitcast.3, f32[6,128,128]{2,1,0:T(8,128)} %refs_3_.1), custom_call_target="tpu_custom_call" | custom-call | tf_op jit(solution)/shard_map/pallas_call | solution.py:328
  29.9 0.0 copy-start
  29.9 1.8 %copy.9 = f32[6,128,128]{2,1,0:T(8,128)} copy(f32[6,128,128]{2,1,0:T(8,128)} %get-tuple-element.4) | data formatting | bytes 786432
  31.7 0.0 copy-done
  31.7 0.7 %copy.10 = f32[2,2,128,128]{3,2,1,0:T(8,128)} copy(f32[2,2,128,128]{3,2,1,0:T(8,128)S(1)} %copy-done) | data formatting | bytes 524288
Async XLA Ops:
  29.9 1.8 %copy-start = (f32[2,2,128,128]{3,2,1,0:T(8,128)S(1)}, f32[2,2,128,128]{3,2,1,0:T(8,128)}, u32[]{:S(2)}) copy-start(f32[2,2,128,128]{3,2,1,0:T(8,128)} %get-tuple-element.5) | copy-start | bytes 786436

commit v3 on v2

--- a/solution.py
+++ b/solution.py
@@ -59,52 +59,53 @@
         copy.start()
 
     barrier = pltpu.get_barrier_semaphore()
-    around = (
-        (left, iy), (right, iy), (ix, up), (ix, down),
-        (left, up), (left, down), (right, up), (right, down),
-    )
+    around = ((left, iy), (right, iy), (ix, up), (ix, down))
     for who in around:
         pl.semaphore_signal(barrier, inc=1, device_id=who, device_id_type=MESH)
 
     lane = lax.broadcasted_iota(jnp.int32, (8, SIDE), 1)
     top, main, low = pl.ds(0, HALO), pl.ds(HALO, SIDE), pl.ds(HALO + SIDE, HALO)
-    first, last = pl.ds(0, HALO), pl.ds(SIDE - HALO, HALO)
+
 
     def rows(k, shift=0):
         return pl.ds(pl.multiple_of(k * 8, 8) + shift, 8)
 
-    def make(stage, plan):
+    def make(stage, base, plan):
         return [
             pltpu.make_async_remote_copy(
                 src_ref=src, dst_ref=dst,
-                send_sem=send.at[stage, n], recv_sem=recv.at[stage, n],
+                send_sem=send.at[stage, base + n], recv_sem=recv.at[stage, base + n],
                 device_id=who, device_id_type=MESH,
             )
             for n, (src, dst, who) in enumerate(plan)
         ]
 
     def halo_copies(h):
-        return make(h, (
+        return make(h, 0, (
             (s.at[h, 0], c[h].at[0, main], (left, iy)),
             (s.at[h, 1], c[h].at[1, main], (right, iy)),
-            (s.at[h, 0, first], c[h].at[0, low], (left, up)),
-            (s.at[h, 0, last], c[h].at[0, top], (left, down)),
-            (s.at[h, 1, first], c[h].at[1, low], (right, up)),
-            (s.at[h, 1, last], c[h].at[1, top], (right, down)),
             (q[h].at[:, pl.ds(HALO, HALO)], q[h].at[:, low], (ix, up)),
             (q[h].at[:, pl.ds(SIDE, HALO)], q[h].at[:, top], (ix, down)),
         ))
 
-    def fold_copies(x):
-        return make(2 + x, (
+    def corner_copies(h):
+        return make(h, 4, (
+            (c[h].at[:, pl.ds(HALO, HALO)], c[h].at[:, low], (ix, up)),
+            (c[h].at[:, pl.ds(SIDE, HALO)], c[h].at[:, top], (ix, down)),
+        ))
+
+    def fold_rows(x):
+        return make(2 + x, 0, (
+            (fp.at[x, :, top], rx.at[x, 0], (ix, up)),
+            (fp.at[x, :, low], rx.at[x, 1], (ix, down)),
+            (f.at[x, :, top], rr.at[x, 0], (ix, up)),
+            (f.at[x, :, low], rr.at[x, 1], (ix, down)),
+        ))
+
+    def fold_columns(x):
+        return make(2 + x, 4, (
             (fp.at[x, 0, main], rc.at[x, 0], (right, iy)),
             (fp.at[x, 1, main], rc.at[x, 1], (left, iy)),
-            (fp.at[x, 0, top], rx.at[x, 0, 0], (right, up)),
-            (fp.at[x, 0, low], rx.at[x, 0, 1], (right, down)),
-            (fp.at[x, 1, top], rx.at[x, 1, 0], (left, up)),
-            (fp.at[x, 1, low], rx.at[x, 1, 1], (left, down)),
-            (f.at[x, :, top], rr.at[x, 0], (ix, up)),
-            (f.at[x, :, low], rr.at[x, 1], (ix, down)),
         ))
 
     right_lanes = [(lane >= PITCH * t) & (lane < PITCH * t + WIDE) for t in range(NT)]
@@ -112,6 +113,29 @@
         (lane >= (PITCH * t - WIDE) % SIDE) & (lane < (PITCH * t - WIDE) % SIDE + WIDE)
         for t in range(NT)
     ]
+
+    def go(copies):
+        for copy in copies:
+            copy.start()
+
+    def arrive(copies):
+        for copy in copies:
+            copy.wait_recv()
+
+    def forward(h, copies):
+        arrive(copies[:2])
+        corners = corner_copies(h)
+        go(corners)
+        return corners
+
+    def relay(x, copies):
+        arrive(copies[:2])
+        for d in range(2):
+            fp[x, d, pl.ds(SIDE, HALO), :] += rx[x, 0, d]
+            fp[x, d, pl.ds(HALO, HALO), :] += rx[x, 1, d]
+        columns = fold_columns(x)
+        go(columns)
+        return columns
 
     def turned(value, amount):
         return value if amount % SIDE == 0 else pltpu.roll(value, amount % SIDE, 1)
@@ -245,9 +269,6 @@
         lax.fori_loop(0, TALL // 8, place, 0)
 
     def fold(x, out):
-        for d in range(2):
-            rc[x, d, last, :] += rx[x, d, 0]
-            rc[x, d, first, :] += rx[x, d, 1]
         for t in range(NT):
             f[x, t, pl.ds(SIDE, HALO), :] += rr[x, 0, t]
             f[x, t, pl.ds(HALO, HALO), :] += rr[x, 1, t]
@@ -269,10 +290,9 @@
 
     loads[0].wait()
     lax.fori_loop(0, SIDE // 8, first_pack, 0)
-    pl.semaphore_wait(barrier, 8)
+    pl.semaphore_wait(barrier, 4)
     halo0 = halo_copies(0)
-    for copy in halo0:
-        copy.start()
+    go(halo0)
 
     lap[:, 0:8, :] = jnp.zeros((4, 8, SIDE), jnp.float32)
     lap[:, SIDE + 8:, :] = jnp.zeros((4, 8, SIDE), jnp.float32)
@@ -286,36 +306,33 @@
     for copy in loads[1:]:
         copy.wait()
     spread(1, cotangent, 0)
-    fold0 = fold_copies(0)
-    for copy in fold0:
-        copy.start()
-
-    for copy in halo0:
-        copy.wait_recv()
+    rows0 = fold_rows(0)
+    go(rows0)
+    corners0 = forward(0, halo0)
+    columns0 = relay(0, rows0)
+
+    arrive(halo0[2:] + corners0)
     make_windows(0)
     advect()
     halo1 = halo_copies(1)
-    for copy in halo1:
-        copy.start()
-
-    for copy in fold0:
-        copy.wait()
+    go(halo1)
+
+    arrive(rows0[2:] + columns0)
     fold(0, ma)
     spread(0, ma, 1)
-    fold1 = fold_copies(1)
-    for copy in fold1:
-        copy.start()
+    rows1 = fold_rows(1)
+    go(rows1)
+    corners1 = forward(1, halo1)
+    columns1 = relay(1, rows1)
     sensitivity(0, ma)
 
-    for copy in halo1:
-        copy.wait_recv()
+    arrive(halo1[2:] + corners1)
     make_windows(1)
     sensitivity(1, cotangent)
 
-    for copy in fold1:
-        copy.wait()
+    arrive(rows1[2:] + columns1)
     fold(1, grad)
-    for copy in halo0 + halo1:
+    for copy in halo0 + corners0 + rows0 + columns0 + halo1 + corners1 + rows1 + columns1:
         copy.wait_send()
 
 

time: 32.6 us -> 37.1 us (1.14)
  Pallas kernels: 29.2 us -> 33.8 us
    pallas_call x1, Pallas kernels: 29.2 us -> 33.8 us  [body(): pl.pallas_call(lambda *refs: kernel(sizes, *refs), out_shape=(jax.ShapeDt...]
where the time goes in v3:
time: 37.1 us; the launch traced here: 36.9 us
  Pallas kernels  33.8 us (91%)
  local copies, waits for them, and re-layouts  2.52 us (7%)
  between operations  0.65 us (2%)
    pallas_call x1, Pallas kernels, body(): pl.pallas_call(lambda *refs: kernel(sizes, *refs), out_shape=(jax.ShapeDt...  33.8 us
    unnamed x4, local copies, waits for them, and re-layouts  2.52 us

profile of v3, /device:TPU:0, one launch (start us, length us, event | category | flops | bytes accessed | tf_op | source)
XLA Modules:
  0.0 36.9 jit_solution(9353925067314052413)
XLA Ops:
  0.6 33.8 %shard_map.59 = (f32[6,128,128]{2,1,0:T(8,128)}, f32[2,2,128,128]{3,2,1,0:T(8,128)}) custom-call(f32[6,128,128]{2,1,0:T(8,128)} %refs_0_.1, f32[2,2,128,128]{3,2,1,0:T(8,128)} %refs_1_.1, s32[2,1,1,2]{3,2,1,0:T(1,128)} %bitcast.3, f32[6,128,128]{2,1,0:T(8,128)} %refs_3_.1), custom_call_target="tpu_custom_call" | custom-call | tf_op jit(solution)/shard_map/pallas_call | solution.py:345
  34.4 0.0 copy-start
  34.4 1.8 %copy.9 = f32[6,128,128]{2,1,0:T(8,128)} copy(f32[6,128,128]{2,1,0:T(8,128)} %get-tuple-element.4) | data formatting | bytes 786432
  36.2 0.0 copy-done
  36.2 0.7 %copy.10 = f32[2,2,128,128]{3,2,1,0:T(8,128)} copy(f32[2,2,128,128]{3,2,1,0:T(8,128)S(1)} %copy-done) | data formatting | bytes 524288
Async XLA Ops:
  34.4 1.8 %copy-start = (f32[2,2,128,128]{3,2,1,0:T(8,128)S(1)}, f32[2,2,128,128]{3,2,1,0:T(8,128)}, u32[]{:S(2)}) copy-start(f32[2,2,128,128]{3,2,1,0:T(8,128)} %get-tuple-element.5) | copy-start | bytes 786436

commit v4 on v2

--- a/solution.py
+++ b/solution.py
@@ -13,6 +13,7 @@
 PITCH = 21
 WIDE = 18
 PAD = 40
+GROUP = 4
 DEEP = 216
 MESH = pl.DeviceIdType.MESH
 
@@ -71,7 +72,21 @@
     first, last = pl.ds(0, HALO), pl.ds(SIDE - HALO, HALO)
 
     def rows(k, shift=0):
-        return pl.ds(pl.multiple_of(k * 8, 8) + shift, 8)
+        return pl.ds((k * 8 if isinstance(k, int) else pl.multiple_of(k * 8, 8)) + shift, 8)
+
+    def loop(count, block):
+        def several(n, _):
+            for j in range(GROUP):
+                block(n * GROUP + j, 0)
+            return 0
+
+        if count >= 2 * GROUP:
+            lax.fori_loop(0, count // GROUP, several, 0)
+            rest = count - count % GROUP
+        else:
+            rest = 0
+        for k in range(rest, count):
+            block(k, 0)
 
     def make(stage, plan):
         return [
@@ -153,7 +168,7 @@
                     w[b, t, rows(k), :] = pltpu.roll(jnp.where(masks[b], mid, side), turns[b], 1)
             return 0
 
-        lax.fori_loop(0, WIN // 8, block, 0)
+        loop(WIN // 8, block)
 
     def advect():
         def block(k, _):
@@ -172,7 +187,7 @@
             s[1, 0, rows(k), :], s[1, 1, rows(k), :] = pack(done)
             return 0
 
-        lax.fori_loop(0, SIDE // 8, block, 0)
+        loop(SIDE // 8, block)
 
     def sensitivity(step, g):
         def block(k, _):
@@ -195,7 +210,7 @@
             sens[step, 1, rows(k), :] = -along_cols
             return 0
 
-        lax.fori_loop(0, SIDE // 8, block, 0)
+        loop(SIDE // 8, block)
 
     def spread(step, g, x):
         dy, base, shifts, masks = geometry(step)
@@ -212,7 +227,7 @@
                     vp[b, t, rows(k, 8), :] = lb[b] * value
             return 0
 
-        lax.fori_loop(0, SIDE // 8, weigh, 0)
+        loop(SIDE // 8, weigh)
 
         def deposit(k, _):
             la = [lap[a, rows(k, 8 - a), :] for a in range(4)]
@@ -231,7 +246,7 @@
             hb[0, rows(k, PAD), :], hb[1, rows(k, PAD), :] = pack(rims)
             return 0
 
-        lax.fori_loop(0, WIN // 8, deposit, 0)
+        loop(WIN // 8, deposit)
         start = PAD - HALO + 2 + dy
 
         def place(k, _):
@@ -242,7 +257,7 @@
                 fp[x, d, rows(k), :] = hb[d, at, :]
             return 0
 
-        lax.fori_loop(0, TALL // 8, place, 0)
+        loop(TALL // 8, place)
 
     def fold(x, out):
         for d in range(2):
@@ -260,7 +275,7 @@
                 out[t, rows(k), :] = f[x, t, rows(k, HALO), :] + low_part + high_part
             return 0
 
-        lax.fori_loop(0, SIDE // 8, block, 0)
+        loop(SIDE // 8, block)
 
     def first_pack(k, _):
         values = [q0[t, rows(k, HALO), :] for t in range(NT)]
@@ -268,7 +283,7 @@
         return 0
 
     loads[0].wait()
-    lax.fori_loop(0, SIDE // 8, first_pack, 0)
+    loop(SIDE // 8, first_pack)
     pl.semaphore_wait(barrier, 8)
     halo0 = halo_copies(0)
     for copy in halo0:

time: 32.6 us -> 30 us (0.920)
  Pallas kernels: 29.2 us -> 26.7 us
    pallas_call x1, Pallas kernels: 29.2 us -> 26.7 us  [body(): pl.pallas_call(lambda *refs: kernel(sizes, *refs), out_shape=(jax.ShapeDt...]
where the time goes in v4:
time: 30 us; the launch traced here: 29.9 us
  Pallas kernels  26.7 us (89%)
  local copies, waits for them, and re-layouts  2.52 us (8%)
  between operations  0.65 us (2%)
    pallas_call x1, Pallas kernels, body(): pl.pallas_call(lambda *refs: kernel(sizes, *refs), out_shape=(jax.ShapeDt...  26.7 us
    unnamed x4, local copies, waits for them, and re-layouts  2.52 us

profile of v4, /device:TPU:0, one launch (start us, length us, event | category | flops | bytes accessed | tf_op | source)
XLA Modules:
  0.0 29.9 jit_solution(17615595521826782283)
XLA Ops:
  0.6 26.7 %shard_map.59 = (f32[6,128,128]{2,1,0:T(8,128)}, f32[2,2,128,128]{3,2,1,0:T(8,128)}) custom-call(f32[6,128,128]{2,1,0:T(8,128)} %refs_0_.1, f32[2,2,128,128]{3,2,1,0:T(8,128)} %refs_1_.1, s32[2,1,1,2]{3,2,1,0:T(1,128)} %bitcast.3, f32[6,128,128]{2,1,0:T(8,128)} %refs_3_.1), custom_call_target="tpu_custom_call" | custom-call | tf_op jit(solution)/shard_map/pallas_call | solution.py:343
  27.3 0.0 copy-start
  27.3 1.8 %copy.9 = f32[6,128,128]{2,1,0:T(8,128)} copy(f32[6,128,128]{2,1,0:T(8,128)} %get-tuple-element.4) | data formatting | bytes 786432
  29.2 0.0 copy-done
  29.2 0.7 %copy.10 = f32[2,2,128,128]{3,2,1,0:T(8,128)} copy(f32[2,2,128,128]{3,2,1,0:T(8,128)S(1)} %copy-done) | data formatting | bytes 524288
Async XLA Ops:
  27.3 1.8 %copy-start = (f32[2,2,128,128]{3,2,1,0:T(8,128)S(1)}, f32[2,2,128,128]{3,2,1,0:T(8,128)}, u32[]{:S(2)}) copy-start(f32[2,2,128,128]{3,2,1,0:T(8,128)} %get-tuple-element.5) | copy-start | bytes 786436

commit v5 on v4

--- a/solution.py
+++ b/solution.py
@@ -39,7 +39,7 @@
 
 def kernel(
     sizes, tracer_in, courant_in, disp_in, cotangent_in, grad, sens,
-    courant, disp, cotangent, q0, q1, s, c0, c1, w, lap, vp, eb, hb, f, fp, ma, rr, rc, rx, send, recv, load,
+    courant, disp, cotangent, q0, q1, s, c0, c1, w, lap, lbp, eb, hb, f, fp, ma, rr, rc, rx, send, recv, load,
 ):
     nx, ny = sizes
     q, c = (q0, q1), (c0, c1)
@@ -53,7 +53,7 @@
             (tracer_in, q0.at[:, pl.ds(HALO, SIDE)]),
             (disp_in, disp),
             (courant_in, courant),
-            (cotangent_in, cotangent),
+            (cotangent_in, cotangent.at[:, pl.ds(8, SIDE)]),
         ))
     ]
     for copy in loads:
@@ -194,7 +194,7 @@
             ty, tx = fractions(step, k)
             la, lb = lagrange_weights(ty), lagrange_weights(tx)
             da, db = lagrange_slopes(ty), lagrange_slopes(tx)
-            gs = [g[t, rows(k), :] for t in range(NT)]
+            gs = [g[t, rows(k, 8), :] for t in range(NT)]
             along_rows = along_cols = None
             for a in range(4):
                 line = slope = None
@@ -221,23 +221,24 @@
             la, lb = lagrange_weights(ty), lagrange_weights(tx)
             for a in range(4):
                 lap[a, rows(k, 8), :] = la[a]
-            for t in range(NT):
-                value = g[t, rows(k), :]
-                for b in range(4):
-                    vp[b, t, rows(k, 8), :] = lb[b] * value
+                lbp[a, rows(k, 8), :] = lb[a]
             return 0
 
         loop(SIDE // 8, weigh)
 
         def deposit(k, _):
-            la = [lap[a, rows(k, 8 - a), :] for a in range(4)]
+            factor = [
+                [lap[a, rows(k, 8 - a), :] * lbp[b, rows(k, 8 - a), :] for a in range(4)]
+                for b in range(4)
+            ]
             rims = []
             for t in range(NT):
+                values = [g[t, rows(k, 8 - a), :] for a in range(4)]
                 mid = rim = jnp.zeros((8, SIDE), jnp.float32)
                 for b in range(4):
-                    total = la[0] * vp[b, t, rows(k, 8), :]
+                    total = factor[b][0] * values[0]
                     for a in range(1, 4):
-                        total = total + la[a] * vp[b, t, rows(k, 8 - a), :]
+                        total = total + factor[b][a] * values[a]
                     moved = pltpu.roll(total, turns[b], 1)
                     mid = mid + jnp.where(masks[b], moved, 0.0)
                     rim = rim + jnp.where(masks[b], 0.0, moved)
@@ -259,7 +260,7 @@
 
         loop(TALL // 8, place)
 
-    def fold(x, out):
+    def fold(x, out, shift):
         for d in range(2):
             rc[x, d, last, :] += rx[x, d, 0]
             rc[x, d, first, :] += rx[x, d, 1]
@@ -272,7 +273,7 @@
             for t in range(NT):
                 low_part = turned(jnp.where(right_lanes[t], from_left, 0.0), -PITCH * t)
                 high_part = turned(jnp.where(left_lanes[t], from_right, 0.0), -PITCH * t)
-                out[t, rows(k), :] = f[x, t, rows(k, HALO), :] + low_part + high_part
+                out[t, rows(k, shift), :] = f[x, t, rows(k, HALO), :] + low_part + high_part
             return 0
 
         loop(SIDE // 8, block)
@@ -291,8 +292,11 @@
 
     lap[:, 0:8, :] = jnp.zeros((4, 8, SIDE), jnp.float32)
     lap[:, SIDE + 8:, :] = jnp.zeros((4, 8, SIDE), jnp.float32)
-    vp[:, :, 0:8, :] = jnp.zeros((4, NT, 8, SIDE), jnp.float32)
-    vp[:, :, SIDE + 8:, :] = jnp.zeros((4, NT, 8, SIDE), jnp.float32)
+    lbp[:, 0:8, :] = jnp.zeros((4, 8, SIDE), jnp.float32)
+    lbp[:, SIDE + 8:, :] = jnp.zeros((4, 8, SIDE), jnp.float32)
+    for g in (cotangent, ma):
+        g[:, 0:8, :] = jnp.zeros((NT, 8, SIDE), jnp.float32)
+        g[:, SIDE + 8:, :] = jnp.zeros((NT, 8, SIDE), jnp.float32)
     eb[:, 0:PAD, :] = jnp.zeros((NT, PAD, SIDE), jnp.float32)
     eb[:, PAD + WIN:, :] = jnp.zeros((NT, DEEP - PAD - WIN, SIDE), jnp.float32)
     hb[:, 0:PAD, :] = jnp.zeros((2, PAD, SIDE), jnp.float32)
@@ -315,7 +319,7 @@
 
     for copy in fold0:
         copy.wait()
-    fold(0, ma)
+    fold(0, ma, 8)
     spread(0, ma, 1)
     fold1 = fold_copies(1)
     for copy in fold1:
@@ -329,7 +333,7 @@
 
     for copy in fold1:
         copy.wait()
-    fold(1, grad)
+    fold(1, grad, 0)
     for copy in halo0 + halo1:
         copy.wait_send()
 
@@ -351,7 +355,7 @@
             scratch_shapes=[
                 pltpu.VMEM((2, 2, SIDE, SIDE), f32),
                 pltpu.SMEM((2, 1, 1, 2), jnp.int32),
-                pltpu.VMEM((NT, SIDE, SIDE), f32),
+                pltpu.VMEM((NT, SIDE + 16, SIDE), f32),
                 pltpu.VMEM((NT, TALL, SIDE), f32),
                 pltpu.VMEM((NT, TALL, SIDE), f32),
                 pltpu.VMEM((2, 2, SIDE, SIDE), f32),
@@ -359,12 +363,12 @@
                 pltpu.VMEM((2, TALL, SIDE), f32),
                 pltpu.VMEM((4, NT, WIN, SIDE), f32),
                 pltpu.VMEM((4, SIDE + 16, SIDE), f32),
-                pltpu.VMEM((4, NT, SIDE + 16, SIDE), f32),
+                pltpu.VMEM((4, SIDE + 16, SIDE), f32),
                 pltpu.VMEM((NT, DEEP, SIDE), f32),
                 pltpu.VMEM((2, DEEP, SIDE), f32),
                 pltpu.VMEM((2, NT, TALL, SIDE), f32),
                 pltpu.VMEM((2, 2, TALL, SIDE), f32),
-                pltpu.VMEM((NT, SIDE, SIDE), f32),
+                pltpu.VMEM((NT, SIDE + 16, SIDE), f32),
                 pltpu.VMEM((2, 2, NT, HALO, SIDE), f32),
                 pltpu.VMEM((2, 2, SIDE, SIDE), f32),
                 pltpu.VMEM((2, 2, 2, HALO, SIDE), f32),

time: 30 us -> 30 us (level)
  no operation moved by 1% of the time
where the time goes in v5:
time: 30 us; the launch traced here: 29.8 us
  Pallas kernels  26.7 us (89%)
  local copies, waits for them, and re-layouts  2.52 us (8%)
  between operations  0.65 us (2%)
    pallas_call x1, Pallas kernels, body(): pl.pallas_call(lambda *refs: kernel(sizes, *refs), out_shape=(jax.ShapeDt...  26.7 us
    unnamed x4, local copies, waits for them, and re-layouts  2.52 us

profile of v5, /device:TPU:0, one launch (start us, length us, event | category | flops | bytes accessed | tf_op | source)
XLA Modules:
  0.0 29.8 jit_solution(318642416318625415)
XLA Ops:
  0.6 26.7 %shard_map.59 = (f32[6,128,128]{2,1,0:T(8,128)}, f32[2,2,128,128]{3,2,1,0:T(8,128)}) custom-call(f32[6,128,128]{2,1,0:T(8,128)} %refs_0_.1, f32[2,2,128,128]{3,2,1,0:T(8,128)} %refs_1_.1, s32[2,1,1,2]{3,2,1,0:T(1,128)} %bitcast.3, f32[6,128,128]{2,1,0:T(8,128)} %refs_3_.1), custom_call_target="tpu_custom_call" | custom-call | tf_op jit(solution)/shard_map/pallas_call | solution.py:347
  27.3 0.0 copy-start
  27.3 1.8 %copy.9 = f32[6,128,128]{2,1,0:T(8,128)} copy(f32[6,128,128]{2,1,0:T(8,128)} %get-tuple-element.4) | data formatting | bytes 786432
  29.1 0.0 copy-done
  29.1 0.7 %copy.10 = f32[2,2,128,128]{3,2,1,0:T(8,128)} copy(f32[2,2,128,128]{3,2,1,0:T(8,128)S(1)} %copy-done) | data formatting | bytes 524288
Async XLA Ops:
  27.3 1.8 %copy-start = (f32[2,2,128,128]{3,2,1,0:T(8,128)S(1)}, f32[2,2,128,128]{3,2,1,0:T(8,128)}, u32[]{:S(2)}) copy-start(f32[2,2,128,128]{3,2,1,0:T(8,128)} %get-tuple-element.5) | copy-start | bytes 786436
